TPU v7x, 32 devices: a whole 2x2x4 slice. The times are simulated.
32 devices in a mesh: slab: 2 (over y), row: 8 (over z, x), col: 2 (over core).
Axes of the slice: x: 2, y: 2, z: 4, core: 2. Of those that a mesh axis runs over, the one named last changes fastest.
Arguments:
- start: float32 [1024, 4096], P(('slab', 'row'), 'col'), parts along dimension 0, may hold values from -5 to 6
- dest_tile: int32 [262144], P(('slab', 'row', 'col')), parts along dimension 0, may hold values from 0 to 15, as said below
- cell_row: int32 [262144], P(('slab', 'row', 'col')), parts along dimension 0, may hold values from 0 to 63
- cell_col: int32 [262144], P(('slab', 'row', 'col')), parts along dimension 0, may hold values from 0 to 2047
- source_type: int32 [262144], P(('slab', 'row', 'col')), parts along dimension 0, may hold values from 0 to 2
- sounding_value: float32 [262144], P(('slab', 'row', 'col')), parts along dimension 0, may hold values from -6 to 6
- sounding_weight: float32 [262144], P(('slab', 'row', 'col')), parts along dimension 0, may hold values from 0.1 to 10
- type_gain: float32 [3], replicated, may hold values from 0.3 to 3
Outputs:
- surface: float32 [1024, 4096], P(('slab', 'row'), 'col'), parts along dimension 0
There are 2 independent parts, one for each index of `slab`. A program takes and returns all parts, laid end to end along the dimension named above; an argument that names none is the same for every part. Nothing has to cross between parts.
Inputs may be any that keep to these rules, and one draw needn't show every extreme that they name: `dest_tile`: each track owner sends at most 640 soundings to any one tile, and in every draw some tile receives exactly 640 from every track owner.
All inputs are finite; a program needn't handle non-finite values.
Results may differ from a plain program's by a relative error of at most 0.0003.
Values sent between devices are 32-bit elements; how exact they have to be, the bound alone decides.
A program may use at most 64 MiB of HBM per device.

v0:
```python
import math

import jax
import jax.numpy as jnp
from jax import lax
from jax.sharding import PartitionSpec as P

SWEEPS = 4


tension = 0.35
centre_weight = 20.0 * (1.0 - tension) + 4.0 * tension
near_weight = 8.0 * (1.0 - tension) + tension
corner_weight = 2.0 * (1.0 - tension)
distant_weight = 1.0 - tension
damping = 0.5


def padded_2(array, sides, width):
    for axis, dim in sides:
        count, length = (lax.axis_size(axis), array.shape[dim])
        up = [(i, (i + 1) % count) for i in range(count - 1)]
        down = [(j, i) for i, j in up]
        last = lax.slice_in_dim(array, length - width, length, axis=dim)
        leading = lax.slice_in_dim(array, 0, width, axis=dim)
        before = lax.ppermute(last, axis, up)
        after = lax.ppermute(leading, axis, down)
        array = jnp.concatenate([before, array, after], axis=dim)
    return array


def neighbour_sums(padded):
    height = padded.shape[0] - 4
    width = padded.shape[1] - 4

    def shifted(down, across):
        return padded[2 + down : 2 + down + height, 2 + across : 2 + across + width]

    centre = shifted(0, 0)
    near = shifted(1, 0) + shifted(-1, 0) + shifted(0, 1) + shifted(0, -1)
    corner = shifted(1, 1) + shifted(1, -1) + shifted(-1, 1) + shifted(-1, -1)
    distant = shifted(2, 0) + shifted(-2, 0) + shifted(0, 2) + shifted(0, -2)
    return (centre, near, corner, distant)


def relax_step(padded, data_weight, data_moment):
    centre, near, corner, distant = neighbour_sums(padded)
    applied = (
        centre_weight * centre
        - near_weight * near
        + corner_weight * corner
        + distant_weight * distant
    )
    return centre + damping * (data_moment - applied - data_weight * centre) / (
        centre_weight + data_weight
    )


def body(
    start, dest_tile, cell_row, cell_col, source_type, sounding_value, sounding_weight, type_gain
):
    tile_rows, tile_cols = start.shape
    row_count = lax.axis_size("row")
    col_count = lax.axis_size("col")
    tile_count = row_count * col_count
    sounding_count = dest_tile.shape[0]
    capacity = 5 * sounding_count // (4 * tile_count)
    factor = jnp.where(
        source_type == 0, type_gain[0], jnp.where(source_type == 1, type_gain[1], type_gain[2])
    )
    scaled = sounding_weight * factor
    moment = scaled * sounding_value
    payload = jnp.stack(
        [scaled, moment, cell_row.astype(jnp.float32), cell_col.astype(jnp.float32)]
    )
    block_rows = math.gcd(sounding_count, 512)
    block_total = sounding_count // block_rows
    tile_ids = jnp.arange(tile_count, dtype=jnp.int32)
    slot_ids = jnp.arange(capacity, dtype=jnp.int32)
    position = jnp.arange(block_rows, dtype=jnp.int32)
    earlier = (position[None, :] < position[:, None]).astype(jnp.bfloat16)

    def tally_block(carry, inputs):
        counts, filled = carry
        dest_block, payload_block = inputs
        hits = dest_block[:, None] == tile_ids[None, :]
        before = (
            jnp.dot(earlier, hits.astype(jnp.bfloat16), preferred_element_type=jnp.float32)
            + counts[None, :]
        )
        tile_onehot = hits.astype(jnp.float32)
        ranking = jnp.sum(before * tile_onehot, axis=1)
        slot_onehot = (
            jnp.abs(ranking[:, None] - slot_ids[None, :].astype(jnp.float32)) < 0.5
        ).astype(jnp.float32)
        placed = payload_block[:, :, None] * slot_onehot[None, :, :]
        filled = filled + jnp.einsum(
            "it,cir->ctr", tile_onehot, placed, precision=lax.Precision.HIGHEST
        )
        return ((counts + jnp.sum(tile_onehot, axis=0), filled), None)

    initial = (
        jnp.zeros((tile_count,), jnp.float32),
        jnp.zeros((4, tile_count, capacity), jnp.float32),
    )
    dest_blocks = dest_tile.reshape(block_total, block_rows)
    payload_blocks = jnp.transpose(payload.reshape(4, block_total, block_rows), (1, 0, 2))
    (final_counts, outgoing), unused = lax.scan(tally_block, initial, (dest_blocks, payload_blocks))
    incoming = lax.all_to_all(outgoing, ("row", "col"), split_axis=1, concat_axis=1, tiled=True)
    incoming = incoming.reshape(4, -1)
    slot_total = incoming.shape[1]
    recv_rows = math.gcd(slot_total, 2048)
    recv_blocks = slot_total // recv_rows
    row_ids = jnp.arange(tile_rows, dtype=jnp.float32)
    col_ids = jnp.arange(tile_cols, dtype=jnp.float32)

    def grid_block(total, block):
        row_onehot = (jnp.abs(block[2][:, None] - row_ids[None, :]) < 0.5).astype(jnp.float32)
        col_onehot = (jnp.abs(block[3][:, None] - col_ids[None, :]) < 0.5).astype(jnp.float32)
        left = jnp.concatenate(
            [row_onehot * block[0][:, None], row_onehot * block[1][:, None]], axis=1
        )
        term = lax.dot_general(
            left,
            col_onehot,
            (((0,), (0,)), ((), ())),
            precision=lax.Precision.HIGHEST,
            preferred_element_type=jnp.float32,
        )
        return (total + term, None)

    slot_blocks = jnp.transpose(incoming.reshape(4, recv_blocks, recv_rows), (1, 0, 2))
    grids, unused_grid = lax.scan(
        grid_block, jnp.zeros((2 * tile_rows, tile_cols), jnp.float32), slot_blocks
    )
    grid_weight = grids[:tile_rows]
    grid_moment = grids[tile_rows:]
    current = start
    for level in range(SWEEPS):
        padded = padded_2(current, (("row", 0), ("col", 1)), 2)
        current = relax_step(padded, grid_weight, grid_moment)
    return current


def solution(mesh):
    in_specs = (
        P(("slab", "row"), "col"),
        P(("slab", "row", "col")),
        P(("slab", "row", "col")),
        P(("slab", "row", "col")),
        P(("slab", "row", "col")),
        P(("slab", "row", "col")),
        P(("slab", "row", "col")),
        P(),
    )
    out_specs = P(("slab", "row"), "col")
    return jax.shard_map(body, mesh=mesh, in_specs=in_specs, out_specs=out_specs, check_vma=False)
```

profile of v0, /device:TPU:13, one launch (start us, length us, event | category | flops | bytes accessed | tf_op | source)
XLA Modules:
  0.0 169.8 jit_solution(1421352669246679886)
XLA Ops:
  0.9 3.0 %collective-permute-start = (f32[2,2048]{1,0:T(2,128)S(1)}, f32[2,2048]{1,0:T(2,128)S(1)}, u32[]{:S(2)}, u32[]{:S(2)}) collective-permute-start(f32[2,2048]{1,0:T(2,128)S(1)} %get-tuple-element.222), channel_id=1, source_target_pairs={{2,0},{4,2},{6,4},{8,6},{10,8},{12,10},{14,12},{3,1},{5,3},{7,5},{... | collective-permute-start | bytes 49160 | tf_op jit(solution)/shard_map/ppermute | solution.py:27
  3.9 2.3 %collective-permute-start.1 = (f32[2,2048]{1,0:T(2,128)S(1)}, f32[2,2048]{1,0:T(2,128)S(1)}, u32[]{:S(2)}, u32[]{:S(2)}) collective-permute-start(f32[2,2048]{1,0:T(2,128)S(1)} %get-tuple-element.223), channel_id=1, source_target_pairs={{0,2},{2,4},{4,6},{6,8},{8,10},{10,12},{12,14},{1,3},{3,5},{5,7},{... | collective-permute-start | bytes 49160 | tf_op jit(solution)/shard_map/ppermute | solution.py:26
  9.9 2.7 %fusion.118 = (f32[8192]{0:T(1024)S(1)}, f32[8192]{0:T(1024)S(1)}) fusion(f32[8192]{0:T(1024)} %param.17, f32[8192]{0:T(1024)} %param.18, f32[]{:T(128)} %bitcast.2, f32[]{:T(128)} %bitcast.1, s32[8192]{0:T(1024)} %param.16, f32[]{:T(128)} %bitcast), kind=kLoop, calls=%fused_computation.183 | loop fusion | flops 49152 | bytes 163852 | tf_op jit(solution)/shard_map/mul | solution.py:72
  12.8 45.2 %while.26 = (s32[]{:T(128)}, f32[16]{0:T(128)S(1)}, f32[4,16,640]{2,1,0:T(8,128)S(1)}, s32[16,512]{1,0:T(8,128)S(1)}, f32[16,4,512]{2,1,0:T(4,128)S(1)}, /*index=5*/s32[]{:T(128)}, s32[]{:T(128)}) while((s32[]{:T(128)}, f32[16]{0:T(128)S(1)}, f32[4,16,640]{2,1,0:T(8,128)S(1)}, s32[16,512]{1,0:T(8,128)S(1)}, ...), condition=%wide.region_3.4_spmd.clone, body=%wide.region_0.3_spmd.clone.sunk | while | flops 263348368 | bytes 2993640 | solution.py:108
  13.5 2.1 %fusion.143 = f32[4,16,640]{2,1,0:T(8,128)S(1)} fusion(f32[512,640]{1,0:T(8,128)S(1)} %fusion.142, f32[4,512]{1,0:T(4,128)S(1)} %dynamic-slice_bitcast_fusion.2, f32[4,16,640]{2,1,0:T(8,128)S(1)} %get-tuple-element.302, pred[]{:T(512)S(6)} %compare.6, s32[512]{0:T(512)S(1)} %bitcast.63), kind=kOutput, calls=%fused_computation.33.clone.1 | convolution fusion | flops 253059072 | bytes 1648641 | tf_op jit(solution)/shard_map/while/body/eval_jaxpr/it,cir->ctr/dot_general | solution.py:97
  16.4 2.1 %fusion.143 = f32[4,16,640]{2,1,0:T(8,128)S(1)} fusion(f32[512,640]{1,0:T(8,128)S(1)} %fusion.142, f32[4,512]{1,0:T(4,128)S(1)} %dynamic-slice_bitcast_fusion.2, f32[4,16,640]{2,1,0:T(8,128)S(1)} %get-tuple-element.302, pred[]{:T(512)S(6)} %compare.6, s32[512]{0:T(512)S(1)} %bitcast.63), kind=kOutput, calls=%fused_computation.33.clone.1 | convolution fusion | flops 253059072 | bytes 1648641 | tf_op jit(solution)/shard_map/while/body/eval_jaxpr/it,cir->ctr/dot_general | solution.py:97
  19.2 2.1 %fusion.143 = f32[4,16,640]{2,1,0:T(8,128)S(1)} fusion(f32[512,640]{1,0:T(8,128)S(1)} %fusion.142, f32[4,512]{1,0:T(4,128)S(1)} %dynamic-slice_bitcast_fusion.2, f32[4,16,640]{2,1,0:T(8,128)S(1)} %get-tuple-element.302, pred[]{:T(512)S(6)} %compare.6, s32[512]{0:T(512)S(1)} %bitcast.63), kind=kOutput, calls=%fused_computation.33.clone.1 | convolution fusion | flops 253059072 | bytes 1648641 | tf_op jit(solution)/shard_map/while/body/eval_jaxpr/it,cir->ctr/dot_general | solution.py:97
  22.0 2.1 %fusion.143 = f32[4,16,640]{2,1,0:T(8,128)S(1)} fusion(f32[512,640]{1,0:T(8,128)S(1)} %fusion.142, f32[4,512]{1,0:T(4,128)S(1)} %dynamic-slice_bitcast_fusion.2, f32[4,16,640]{2,1,0:T(8,128)S(1)} %get-tuple-element.302, pred[]{:T(512)S(6)} %compare.6, s32[512]{0:T(512)S(1)} %bitcast.63), kind=kOutput, calls=%fused_computation.33.clone.1 | convolution fusion | flops 253059072 | bytes 1648641 | tf_op jit(solution)/shard_map/while/body/eval_jaxpr/it,cir->ctr/dot_general | solution.py:97
  24.8 2.1 %fusion.143 = f32[4,16,640]{2,1,0:T(8,128)S(1)} fusion(f32[512,640]{1,0:T(8,128)S(1)} %fusion.142, f32[4,512]{1,0:T(4,128)S(1)} %dynamic-slice_bitcast_fusion.2, f32[4,16,640]{2,1,0:T(8,128)S(1)} %get-tuple-element.302, pred[]{:T(512)S(6)} %compare.6, s32[512]{0:T(512)S(1)} %bitcast.63), kind=kOutput, calls=%fused_computation.33.clone.1 | convolution fusion | flops 253059072 | bytes 1648641 | tf_op jit(solution)/shard_map/while/body/eval_jaxpr/it,cir->ctr/dot_general | solution.py:97
  27.7 2.1 %fusion.143 = f32[4,16,640]{2,1,0:T(8,128)S(1)} fusion(f32[512,640]{1,0:T(8,128)S(1)} %fusion.142, f32[4,512]{1,0:T(4,128)S(1)} %dynamic-slice_bitcast_fusion.2, f32[4,16,640]{2,1,0:T(8,128)S(1)} %get-tuple-element.302, pred[]{:T(512)S(6)} %compare.6, s32[512]{0:T(512)S(1)} %bitcast.63), kind=kOutput, calls=%fused_computation.33.clone.1 | convolution fusion | flops 253059072 | bytes 1648641 | tf_op jit(solution)/shard_map/while/body/eval_jaxpr/it,cir->ctr/dot_general | solution.py:97
  30.5 2.1 %fusion.143 = f32[4,16,640]{2,1,0:T(8,128)S(1)} fusion(f32[512,640]{1,0:T(8,128)S(1)} %fusion.142, f32[4,512]{1,0:T(4,128)S(1)} %dynamic-slice_bitcast_fusion.2, f32[4,16,640]{2,1,0:T(8,128)S(1)} %get-tuple-element.302, pred[]{:T(512)S(6)} %compare.6, s32[512]{0:T(512)S(1)} %bitcast.63), kind=kOutput, calls=%fused_computation.33.clone.1 | convolution fusion | flops 253059072 | bytes 1648641 | tf_op jit(solution)/shard_map/while/body/eval_jaxpr/it,cir->ctr/dot_general | solution.py:97
  33.3 2.1 %fusion.143 = f32[4,16,640]{2,1,0:T(8,128)S(1)} fusion(f32[512,640]{1,0:T(8,128)S(1)} %fusion.142, f32[4,512]{1,0:T(4,128)S(1)} %dynamic-slice_bitcast_fusion.2, f32[4,16,640]{2,1,0:T(8,128)S(1)} %get-tuple-element.302, pred[]{:T(512)S(6)} %compare.6, s32[512]{0:T(512)S(1)} %bitcast.63), kind=kOutput, calls=%fused_computation.33.clone.1 | convolution fusion | flops 253059072 | bytes 1648641 | tf_op jit(solution)/shard_map/while/body/eval_jaxpr/it,cir->ctr/dot_general | solution.py:97
  36.1 2.1 %fusion.143 = f32[4,16,640]{2,1,0:T(8,128)S(1)} fusion(f32[512,640]{1,0:T(8,128)S(1)} %fusion.142, f32[4,512]{1,0:T(4,128)S(1)} %dynamic-slice_bitcast_fusion.2, f32[4,16,640]{2,1,0:T(8,128)S(1)} %get-tuple-element.302, pred[]{:T(512)S(6)} %compare.6, s32[512]{0:T(512)S(1)} %bitcast.63), kind=kOutput, calls=%fused_computation.33.clone.1 | convolution fusion | flops 253059072 | bytes 1648641 | tf_op jit(solution)/shard_map/while/body/eval_jaxpr/it,cir->ctr/dot_general | solution.py:97
  41.8 2.1 %fusion.143 = f32[4,16,640]{2,1,0:T(8,128)S(1)} fusion(f32[512,640]{1,0:T(8,128)S(1)} %fusion.142, f32[4,512]{1,0:T(4,128)S(1)} %dynamic-slice_bitcast_fusion.2, f32[4,16,640]{2,1,0:T(8,128)S(1)} %get-tuple-element.302, pred[]{:T(512)S(6)} %compare.6, s32[512]{0:T(512)S(1)} %bitcast.63), kind=kOutput, calls=%fused_computation.33.clone.1 | convolution fusion | flops 253059072 | bytes 1648641 | tf_op jit(solution)/shard_map/while/body/eval_jaxpr/it,cir->ctr/dot_general | solution.py:97
  47.4 2.1 %fusion.143 = f32[4,16,640]{2,1,0:T(8,128)S(1)} fusion(f32[512,640]{1,0:T(8,128)S(1)} %fusion.142, f32[4,512]{1,0:T(4,128)S(1)} %dynamic-slice_bitcast_fusion.2, f32[4,16,640]{2,1,0:T(8,128)S(1)} %get-tuple-element.302, pred[]{:T(512)S(6)} %compare.6, s32[512]{0:T(512)S(1)} %bitcast.63), kind=kOutput, calls=%fused_computation.33.clone.1 | convolution fusion | flops 253059072 | bytes 1648641 | tf_op jit(solution)/shard_map/while/body/eval_jaxpr/it,cir->ctr/dot_general | solution.py:97
  58.7 7.0 %all-to-all-start = ((f32[4,16,640]{2,0,1:T(4,128)}), f32[4,16,640]{2,0,1:T(4,128)}, u32[]{:S(2)}, u32[]{:S(2)}) async-start(f32[4,16,640]{2,0,1:T(4,128)} %copy.10), calls=%async_computation | async-start | bytes 327680 | tf_op jit(solution)/shard_map/all_to_all | solution.py:109
  65.9 2.3 %collective-permute-start.2 = (f32[68,2]{1,0:T(8,128)S(1)}, f32[68,2]{1,0:T(8,128)S(1)}, u32[]{:S(2)}, u32[]{:S(2)}) collective-permute-start(f32[68,2]{1,0:T(8,128)S(1)} %get-tuple-element.214), channel_id=1, source_target_pairs={{1,0},{3,2},{5,4},{7,6},{9,8},{11,10},{13,12},{15,14},{17,16},{19,... | collective-permute-start | bytes 1640 | tf_op jit(solution)/shard_map/ppermute | solution.py:27
  75.6 44.0 %while.27 = (s32[]{:T(128)}, f32[128,2048]{1,0:T(8,128)S(1)}, f32[5,4,2048]{2,0,1:T(8,128)}, s32[]{:T(128)}, s32[]{:T(128)}, /*index=5*/s32[]{}, s32[]{}, s32[]{}) while((s32[]{:T(128)}, f32[128,2048]{1,0:T(8,128)S(1)}, f32[5,4,2048]{2,0,1:T(8,128)}, s32[]{:T(128)}, s32[]{:T(128)}, /*index=5*/s32[]{}, s32[]{}, s32[]{}) %tuple.80), condition=%wide.region_5.6_spmd.clone, body=%wide.region_4.5_spmd.clone.sunk | while | flops 6456475648 | bytes 4292763 | solution.py:133
  77.5 6.9 %fusion.147 = f32[128,2048]{1,0:T(8,128)S(1)} fusion(f32[2048]{0:T(1024)S(1)} %bitcast.60, f32[2048,64]{1,0:T(8,128)S(1)} %get-tuple-element.291, f32[2048,64]{1,0:T(8,128)S(1)} %get-tuple-element.292, f32[128,2048]{1,0:T(8,128)S(1)} %get-tuple-element.323, pred[]{:T(512)S(6)} %compare.7), kind=kOutput, calls=%fused_computation.11.clone.1 | convolution fusion | flops 6455820288 | bytes 3153921 | tf_op jit(solution)/shard_map/while/body/eval_jaxpr/dot_general | solution.py:123
  86.3 6.9 %fusion.147 = f32[128,2048]{1,0:T(8,128)S(1)} fusion(f32[2048]{0:T(1024)S(1)} %bitcast.60, f32[2048,64]{1,0:T(8,128)S(1)} %get-tuple-element.291, f32[2048,64]{1,0:T(8,128)S(1)} %get-tuple-element.292, f32[128,2048]{1,0:T(8,128)S(1)} %get-tuple-element.323, pred[]{:T(512)S(6)} %compare.7), kind=kOutput, calls=%fused_computation.11.clone.1 | convolution fusion | flops 6455820288 | bytes 3153921 | tf_op jit(solution)/shard_map/while/body/eval_jaxpr/dot_general | solution.py:123
  95.1 6.9 %fusion.147 = f32[128,2048]{1,0:T(8,128)S(1)} fusion(f32[2048]{0:T(1024)S(1)} %bitcast.60, f32[2048,64]{1,0:T(8,128)S(1)} %get-tuple-element.291, f32[2048,64]{1,0:T(8,128)S(1)} %get-tuple-element.292, f32[128,2048]{1,0:T(8,128)S(1)} %get-tuple-element.323, pred[]{:T(512)S(6)} %compare.7), kind=kOutput, calls=%fused_computation.11.clone.1 | convolution fusion | flops 6455820288 | bytes 3153921 | tf_op jit(solution)/shard_map/while/body/eval_jaxpr/dot_general | solution.py:123
  103.9 6.9 %fusion.147 = f32[128,2048]{1,0:T(8,128)S(1)} fusion(f32[2048]{0:T(1024)S(1)} %bitcast.60, f32[2048,64]{1,0:T(8,128)S(1)} %get-tuple-element.291, f32[2048,64]{1,0:T(8,128)S(1)} %get-tuple-element.292, f32[128,2048]{1,0:T(8,128)S(1)} %get-tuple-element.323, pred[]{:T(512)S(6)} %compare.7), kind=kOutput, calls=%fused_computation.11.clone.1 | convolution fusion | flops 6455820288 | bytes 3153921 | tf_op jit(solution)/shard_map/while/body/eval_jaxpr/dot_general | solution.py:123
  112.7 6.9 %fusion.147 = f32[128,2048]{1,0:T(8,128)S(1)} fusion(f32[2048]{0:T(1024)S(1)} %bitcast.60, f32[2048,64]{1,0:T(8,128)S(1)} %get-tuple-element.291, f32[2048,64]{1,0:T(8,128)S(1)} %get-tuple-element.292, f32[128,2048]{1,0:T(8,128)S(1)} %get-tuple-element.323, pred[]{:T(512)S(6)} %compare.7), kind=kOutput, calls=%fused_computation.11.clone.1 | convolution fusion | flops 6455820288 | bytes 3153921 | tf_op jit(solution)/shard_map/while/body/eval_jaxpr/dot_general | solution.py:123
  120.8 2.9 %collective-permute-start.4 = (f32[2,2048]{1,0:T(2,128)S(1)}, f32[2,2048]{1,0:T(2,128)S(1)}, u32[]{:S(2)}, u32[]{:S(2)}) collective-permute-start(f32[2,2048]{1,0:T(2,128)S(1)} %get-tuple-element.220), channel_id=1, source_target_pairs={{2,0},{4,2},{6,4},{8,6},{10,8},{12,10},{14,12},{3,1},{5,3},{7,5},{... | collective-permute-start | bytes 49160 | tf_op jit(solution)/shard_map/ppermute | solution.py:27
  123.7 2.4 %collective-permute-start.5 = (f32[2,2048]{1,0:T(2,128)S(1)}, f32[2,2048]{1,0:T(2,128)S(1)}, u32[]{:S(2)}, u32[]{:S(2)}) collective-permute-start(f32[2,2048]{1,0:T(2,128)S(1)} %get-tuple-element.221), channel_id=1, source_target_pairs={{0,2},{2,4},{4,6},{6,8},{8,10},{10,12},{12,14},{1,3},{3,5},{5,7},{... | collective-permute-start | bytes 49160 | tf_op jit(solution)/shard_map/ppermute | solution.py:26
  126.1 3.0 %collective-permute-done.5 = f32[2,2048]{1,0:T(2,128)S(1)} collective-permute-done((f32[2,2048]{1,0:T(2,128)S(1)}, f32[2,2048]{1,0:T(2,128)S(1)}, u32[]{:S(2)}, u32[]{:S(2)}) %collective-permute-start.5) | collective-permute-done | bytes 16416 | tf_op jit(solution)/shard_map/ppermute | solution.py:26
  129.2 3.1 %collective-permute-start.6 = (f32[68,2]{1,0:T(8,128)S(1)}, f32[68,2]{1,0:T(8,128)S(1)}, u32[]{:S(2)}, u32[]{:S(2)}) collective-permute-start(f32[68,2]{1,0:T(8,128)S(1)} %get-tuple-element.210), channel_id=1, source_target_pairs={{1,0},{3,2},{5,4},{7,6},{9,8},{11,10},{13,12},{15,14},{17,16},{19,... | collective-permute-start | bytes 1640 | tf_op jit(solution)/shard_map/ppermute | solution.py:27
  136.8 3.5 %collective-permute-start.8 = (f32[2,2048]{1,0:T(2,128)S(1)}, f32[2,2048]{1,0:T(2,128)S(1)}, u32[]{:S(2)}, u32[]{:S(2)}) collective-permute-start(f32[2,2048]{1,0:T(2,128)S(1)} %get-tuple-element.218), channel_id=1, source_target_pairs={{2,0},{4,2},{6,4},{8,6},{10,8},{12,10},{14,12},{3,1},{5,3},{7,5},{... | collective-permute-start | bytes 49160 | tf_op jit(solution)/shard_map/ppermute | solution.py:27
  142.3 3.4 %collective-permute-done.9 = f32[2,2048]{1,0:T(2,128)S(1)} collective-permute-done((f32[2,2048]{1,0:T(2,128)S(1)}, f32[2,2048]{1,0:T(2,128)S(1)}, u32[]{:S(2)}, u32[]{:S(2)}) %collective-permute-start.9) | collective-permute-done | bytes 16416 | tf_op jit(solution)/shard_map/ppermute | solution.py:26
  145.8 3.5 %collective-permute-start.10 = (f32[68,2]{1,0:T(8,128)S(1)}, f32[68,2]{1,0:T(8,128)S(1)}, u32[]{:S(2)}, u32[]{:S(2)}) collective-permute-start(f32[68,2]{1,0:T(8,128)S(1)} %get-tuple-element.206), channel_id=1, source_target_pairs={{1,0},{3,2},{5,4},{7,6},{9,8},{11,10},{13,12},{15,14},{17,16},{19,... | collective-permute-start | bytes 1640 | tf_op jit(solution)/shard_map/ppermute | solution.py:27
  155.8 3.4 %collective-permute-start.13 = (f32[2,2048]{1,0:T(2,128)S(1)}, f32[2,2048]{1,0:T(2,128)S(1)}, u32[]{:S(2)}, u32[]{:S(2)}) collective-permute-start(f32[2,2048]{1,0:T(2,128)S(1)} %get-tuple-element.217), channel_id=1, source_target_pairs={{0,2},{2,4},{4,6},{6,8},{8,10},{10,12},{12,14},{1,3},{3,5},{5,7},{... | collective-permute-start | bytes 49160 | tf_op jit(solution)/shard_map/ppermute | solution.py:26
  161.3 3.2 %collective-permute-start.14 = (f32[68,2]{1,0:T(8,128)S(1)}, f32[68,2]{1,0:T(8,128)S(1)}, u32[]{:S(2)}, u32[]{:S(2)}) collective-permute-start(f32[68,2]{1,0:T(8,128)S(1)} %get-tuple-element.202), channel_id=1, source_target_pairs={{1,0},{3,2},{5,4},{7,6},{9,8},{11,10},{13,12},{15,14},{17,16},{19,... | collective-permute-start | bytes 1640 | tf_op jit(solution)/shard_map/ppermute | solution.py:27
  (179 shorter events, 65.1 us)
Async XLA Ops:
  0.9 64.9 %collective-permute-start = (f32[2,2048]{1,0:T(2,128)S(1)}, f32[2,2048]{1,0:T(2,128)S(1)}, u32[]{:S(2)}, u32[]{:S(2)}) collective-permute-start(f32[2,2048]{1,0:T(2,128)S(1)} %get-tuple-element.222), channel_id=1, source_target_pairs={{2,0},{4,2},{6,4},{8,6},{10,8},{12,10},{14,12},{3,1},{5,3},{7,5},{... | collective-permute-start | bytes 49160 | tf_op jit(solution)/shard_map/ppermute | solution.py:27
  3.9 61.9 %collective-permute-start.1 = (f32[2,2048]{1,0:T(2,128)S(1)}, f32[2,2048]{1,0:T(2,128)S(1)}, u32[]{:S(2)}, u32[]{:S(2)}) collective-permute-start(f32[2,2048]{1,0:T(2,128)S(1)} %get-tuple-element.223), channel_id=1, source_target_pairs={{0,2},{2,4},{4,6},{6,8},{8,10},{10,12},{12,14},{1,3},{3,5},{5,7},{... | collective-permute-start | bytes 49160 | tf_op jit(solution)/shard_map/ppermute | solution.py:26
  12.8 53.0 %copy-start = (f32[64,2048]{1,0:T(8,128)S(1)}, f32[64,2048]{1,0:T(8,128)}, u32[]{:S(2)}) copy-start(f32[64,2048]{1,0:T(8,128)} %param.12) | copy-start | bytes 1572868
  58.7 13.7 %all-to-all-start = ((f32[4,16,640]{2,0,1:T(4,128)}), f32[4,16,640]{2,0,1:T(4,128)}, u32[]{:S(2)}, u32[]{:S(2)}) async-start(f32[4,16,640]{2,0,1:T(4,128)} %copy.10), calls=%async_computation | async-start | bytes 327680 | tf_op jit(solution)/shard_map/all_to_all | solution.py:109
  65.9 3.8 %collective-permute-start.2 = (f32[68,2]{1,0:T(8,128)S(1)}, f32[68,2]{1,0:T(8,128)S(1)}, u32[]{:S(2)}, u32[]{:S(2)}) collective-permute-start(f32[68,2]{1,0:T(8,128)S(1)} %get-tuple-element.214), channel_id=1, source_target_pairs={{1,0},{3,2},{5,4},{7,6},{9,8},{11,10},{13,12},{15,14},{17,16},{19,... | collective-permute-start | bytes 1640 | tf_op jit(solution)/shard_map/ppermute | solution.py:27
  68.2 3.1 %collective-permute-start.3 = (f32[68,2]{1,0:T(8,128)S(1)}, f32[68,2]{1,0:T(8,128)S(1)}, u32[]{:S(2)}, u32[]{:S(2)}) collective-permute-start(f32[68,2]{1,0:T(8,128)S(1)} %get-tuple-element.215), channel_id=1, source_target_pairs={{0,1},{2,3},{4,5},{6,7},{8,9},{10,11},{12,13},{14,15},{16,17},{18,... | collective-permute-start | bytes 1640 | tf_op jit(solution)/shard_map/ppermute | solution.py:26
  120.8 5.3 %collective-permute-start.4 = (f32[2,2048]{1,0:T(2,128)S(1)}, f32[2,2048]{1,0:T(2,128)S(1)}, u32[]{:S(2)}, u32[]{:S(2)}) collective-permute-start(f32[2,2048]{1,0:T(2,128)S(1)} %get-tuple-element.220), channel_id=1, source_target_pairs={{2,0},{4,2},{6,4},{8,6},{10,8},{12,10},{14,12},{3,1},{5,3},{7,5},{... | collective-permute-start | bytes 49160 | tf_op jit(solution)/shard_map/ppermute | solution.py:27
  123.7 5.4 %collective-permute-start.5 = (f32[2,2048]{1,0:T(2,128)S(1)}, f32[2,2048]{1,0:T(2,128)S(1)}, u32[]{:S(2)}, u32[]{:S(2)}) collective-permute-start(f32[2,2048]{1,0:T(2,128)S(1)} %get-tuple-element.221), channel_id=1, source_target_pairs={{0,2},{2,4},{4,6},{6,8},{8,10},{10,12},{12,14},{1,3},{3,5},{5,7},{... | collective-permute-start | bytes 49160 | tf_op jit(solution)/shard_map/ppermute | solution.py:26
  129.2 4.4 %collective-permute-start.6 = (f32[68,2]{1,0:T(8,128)S(1)}, f32[68,2]{1,0:T(8,128)S(1)}, u32[]{:S(2)}, u32[]{:S(2)}) collective-permute-start(f32[68,2]{1,0:T(8,128)S(1)} %get-tuple-element.210), channel_id=1, source_target_pairs={{1,0},{3,2},{5,4},{7,6},{9,8},{11,10},{13,12},{15,14},{17,16},{19,... | collective-permute-start | bytes 1640 | tf_op jit(solution)/shard_map/ppermute | solution.py:27
  132.3 3.1 %collective-permute-start.7 = (f32[68,2]{1,0:T(8,128)S(1)}, f32[68,2]{1,0:T(8,128)S(1)}, u32[]{:S(2)}, u32[]{:S(2)}) collective-permute-start(f32[68,2]{1,0:T(8,128)S(1)} %get-tuple-element.211), channel_id=1, source_target_pairs={{0,1},{2,3},{4,5},{6,7},{8,9},{10,11},{12,13},{14,15},{16,17},{18,... | collective-permute-start | bytes 1640 | tf_op jit(solution)/shard_map/ppermute | solution.py:26
  136.8 5.5 %collective-permute-start.8 = (f32[2,2048]{1,0:T(2,128)S(1)}, f32[2,2048]{1,0:T(2,128)S(1)}, u32[]{:S(2)}, u32[]{:S(2)}) collective-permute-start(f32[2,2048]{1,0:T(2,128)S(1)} %get-tuple-element.218), channel_id=1, source_target_pairs={{2,0},{4,2},{6,4},{8,6},{10,8},{12,10},{14,12},{3,1},{5,3},{7,5},{... | collective-permute-start | bytes 49160 | tf_op jit(solution)/shard_map/ppermute | solution.py:27
  140.4 5.4 %collective-permute-start.9 = (f32[2,2048]{1,0:T(2,128)S(1)}, f32[2,2048]{1,0:T(2,128)S(1)}, u32[]{:S(2)}, u32[]{:S(2)}) collective-permute-start(f32[2,2048]{1,0:T(2,128)S(1)} %get-tuple-element.219), channel_id=1, source_target_pairs={{0,2},{2,4},{4,6},{6,8},{8,10},{10,12},{12,14},{1,3},{3,5},{5,7},{... | collective-permute-start | bytes 49160 | tf_op jit(solution)/shard_map/ppermute | solution.py:26
  145.8 5.0 %collective-permute-start.10 = (f32[68,2]{1,0:T(8,128)S(1)}, f32[68,2]{1,0:T(8,128)S(1)}, u32[]{:S(2)}, u32[]{:S(2)}) collective-permute-start(f32[68,2]{1,0:T(8,128)S(1)} %get-tuple-element.206), channel_id=1, source_target_pairs={{1,0},{3,2},{5,4},{7,6},{9,8},{11,10},{13,12},{15,14},{17,16},{19,... | collective-permute-start | bytes 1640 | tf_op jit(solution)/shard_map/ppermute | solution.py:27
  149.3 3.1 %collective-permute-start.11 = (f32[68,2]{1,0:T(8,128)S(1)}, f32[68,2]{1,0:T(8,128)S(1)}, u32[]{:S(2)}, u32[]{:S(2)}) collective-permute-start(f32[68,2]{1,0:T(8,128)S(1)} %get-tuple-element.207), channel_id=1, source_target_pairs={{0,1},{2,3},{4,5},{6,7},{8,9},{10,11},{12,13},{14,15},{16,17},{18,... | collective-permute-start | bytes 1640 | tf_op jit(solution)/shard_map/ppermute | solution.py:26
  153.9 5.3 %collective-permute-start.12 = (f32[2,2048]{1,0:T(2,128)S(1)}, f32[2,2048]{1,0:T(2,128)S(1)}, u32[]{:S(2)}, u32[]{:S(2)}) collective-permute-start(f32[2,2048]{1,0:T(2,128)S(1)} %get-tuple-element.216), channel_id=1, source_target_pairs={{2,0},{4,2},{6,4},{8,6},{10,8},{12,10},{14,12},{3,1},{5,3},{7,5},{... | collective-permute-start | bytes 49160 | tf_op jit(solution)/shard_map/ppermute | solution.py:27
  155.8 5.4 %collective-permute-start.13 = (f32[2,2048]{1,0:T(2,128)S(1)}, f32[2,2048]{1,0:T(2,128)S(1)}, u32[]{:S(2)}, u32[]{:S(2)}) collective-permute-start(f32[2,2048]{1,0:T(2,128)S(1)} %get-tuple-element.217), channel_id=1, source_target_pairs={{0,2},{2,4},{4,6},{6,8},{8,10},{10,12},{12,14},{1,3},{3,5},{5,7},{... | collective-permute-start | bytes 49160 | tf_op jit(solution)/shard_map/ppermute | solution.py:26
  161.3 4.5 %collective-permute-start.14 = (f32[68,2]{1,0:T(8,128)S(1)}, f32[68,2]{1,0:T(8,128)S(1)}, u32[]{:S(2)}, u32[]{:S(2)}) collective-permute-start(f32[68,2]{1,0:T(8,128)S(1)} %get-tuple-element.202), channel_id=1, source_target_pairs={{1,0},{3,2},{5,4},{7,6},{9,8},{11,10},{13,12},{15,14},{17,16},{19,... | collective-permute-start | bytes 1640 | tf_op jit(solution)/shard_map/ppermute | solution.py:27
  164.5 3.1 %collective-permute-start.15 = (f32[68,2]{1,0:T(8,128)S(1)}, f32[68,2]{1,0:T(8,128)S(1)}, u32[]{:S(2)}, u32[]{:S(2)}) collective-permute-start(f32[68,2]{1,0:T(8,128)S(1)} %get-tuple-element.203), channel_id=1, source_target_pairs={{0,1},{2,3},{4,5},{6,7},{8,9},{10,11},{12,13},{14,15},{16,17},{18,... | collective-permute-start | bytes 1640 | tf_op jit(solution)/shard_map/ppermute | solution.py:26
where the time goes:
time: 171 us; the launch traced here: 170 us
  matrix products  72.3 us (42%)
  starting transfers between devices  46 us (27%)
  other arithmetic  21.7 us (13%)
  waiting for transfers between devices  16 us (9%)
  local copies, waits for them, and re-layouts  12.4 us (7%)
    dot_general x5, matrix products, grid_block(): lax.dot_general(left, col_onehot, (((0,), (0,)), ((), ())), precision=lax...  34.6 us
    dot_general x16, matrix products, tally_block(): jnp.einsum('it,cir->ctr', tile_onehot, placed, precision=lax.Precision.HI...  33.5 us
    ppermute x8, starting transfers between devices, padded_2(): after = lax.ppermute(leading, axis, down)  23.5 us
    ppermute x8, starting transfers between devices, padded_2(): before = lax.ppermute(last, axis, up)  15.5 us
    ppermute x8, waiting for transfers between devices, padded_2(): before = lax.ppermute(last, axis, up)  15.2 us
    all_to_all x1, starting transfers between devices, body(): lax.all_to_all(outgoing, ('row', 'col'), split_axis=1, concat_axis=1, til...  7.03 us
    add x4, other arithmetic, relax_step(): centre + damping * (data_moment - applied - data_weight * centre) / (cent...  5.3 us
    slice x5, local copies, waits for them, and re-layouts, grid_block(): block[0][:, None]  4.88 us
  transfers between devices with their start and end apart: 17, of which 8 were waited for; matrix products, arithmetic and copies ran while one was open for 31% of the time, Pallas kernels for 0%

commit v1 on v0

v1 whole, which is shorter than its diff:
```python
import functools

import jax
import jax.numpy as jnp
from jax import lax
from jax.experimental import pallas as pl
from jax.experimental.pallas import tpu as pltpu
from jax.sharding import PartitionSpec as P

SWEEPS = 4
LANES = 128
HALO = 2 * SWEEPS
MARGIN = 8
MESH = pl.DeviceIdType.MESH

tension = 0.35
centre_weight = 20.0 * (1.0 - tension) + 4.0 * tension
near_weight = 8.0 * (1.0 - tension) + tension
corner_weight = 2.0 * (1.0 - tension)
distant_weight = 1.0 - tension
damping = 0.5

f32 = jnp.float32
bf16 = jnp.bfloat16
NT = (((1,), (1,)), ((), ()))


def two_pieces(x):
    high = x.astype(bf16).astype(f32)
    return high, x - high


def kernel(
    row_count, blocks, start, dest, cell_row, cell_col, source, value, weight, gain, out,
    outbox, inbox, left_route, right_route, routed, slots, pieces, left, right, total,
    field, grid, send_sem, recv_sem, halo_send, halo_recv, grid_send, grid_recv,
):
    tile_rows, tile_cols = start.shape
    sounding_rows = dest.shape[0]
    tiles = 2 * row_count
    my_row, my_col = lax.axis_index("row"), lax.axis_index("col")
    me = 2 * my_row + my_col
    other = 1 - my_col
    ext_rows = tile_rows + 2 * HALO
    interior = pl.ds(MARGIN + HALO, tile_rows)

    barrier = pltpu.get_barrier_semaphore()

    def greet(step, carry):
        peer = lax.rem(me + step, tiles)
        pl.semaphore_signal(
            barrier, inc=1, device_id={"row": peer // 2, "col": lax.rem(peer, 2)},
            device_id_type=MESH,
        )
        return carry

    lax.fori_loop(1, tiles, greet, 0)

    destination = dest[...]
    lane_a = lax.broadcasted_iota(jnp.int32, (LANES, 2 * LANES), 0)
    lane_b = lax.broadcasted_iota(jnp.int32, (LANES, 2 * LANES), 1)
    before = jnp.where((lane_a < lane_b) | (lane_b >= LANES), 1.0, 0.0).astype(bf16)
    sub_a = lax.broadcasted_iota(jnp.int32, (sounding_rows, sounding_rows), 0)
    sub_b = lax.broadcasted_iota(jnp.int32, (sounding_rows, sounding_rows), 1)
    above = jnp.where(sub_b < sub_a, 1.0, 0.0).astype(bf16)

    def rank_of(tile, rank):
        hit = jnp.where(destination == tile, 1.0, 0.0)
        both = jnp.dot(hit.astype(bf16), before, preferred_element_type=f32)
        earlier = jnp.dot(
            above, both[:, LANES:].astype(bf16), preferred_element_type=f32
        )
        return rank + hit * (both[:, :LANES] + earlier)

    rank = jnp.zeros(destination.shape, f32)
    if tiles <= 16:
        for tile in range(tiles):
            rank = rank_of(tile, rank)
    else:
        rank = lax.fori_loop(0, tiles, rank_of, rank)
    rank = rank.astype(jnp.int32)
    slots[0] = (destination >> 1) * blocks + (rank >> 7)
    slots[1] = (destination & 1) * LANES + (rank & (LANES - 1))
    kind = source[...]
    factor = jnp.where(kind == 0, gain[0], jnp.where(kind == 1, gain[1], gain[2]))
    scaled = weight[...] * factor
    moment = scaled * value[...]
    pieces[0], pieces[1] = two_pieces(scaled)
    pieces[2], pieces[3] = two_pieces(moment)
    column = cell_col[...]
    pieces[4] = (cell_row[...] * 4 + (column >> 9)).astype(f32)
    pieces[5] = ((column & 511) - 256).astype(f32)

    slot_rows = row_count * blocks
    slot_ids = lax.broadcasted_iota(jnp.int32, (slot_rows, LANES), 0)
    lane_ids = lax.broadcasted_iota(jnp.int32, (2 * LANES, LANES), 0)
    routed[...] = jnp.zeros(routed.shape, f32)

    def place(step, carry):
        for r in range(8):
            here = pl.ds(step * 8 + r, 1)
            lanes = slice(r * LANES, (r + 1) * LANES)
            chosen = slot_ids == slots[0, here, :]
            left_route[:, lanes] = jnp.concatenate(
                [jnp.where(chosen, pieces[p, here, :], 0.0) for p in range(6)], axis=0
            ).astype(bf16)
            right_route[:, lanes] = jnp.where(
                lane_ids == slots[1, here, :], 1.0, 0.0
            ).astype(bf16)
        routed[...] += lax.dot_general(
            left_route[...], right_route[...], NT, preferred_element_type=f32
        )
        return carry

    lax.fori_loop(0, sounding_rows // 8, place, 0)

    def piece(p):
        return routed[p * slot_rows : (p + 1) * slot_rows, :]

    packed = piece(4)
    placed_row = jnp.floor(packed * 0.25)
    placed_col = (packed - 4.0 * placed_row) * 512.0 + (piece(5) + 256.0)
    values = (piece(0) + piece(1), piece(2) + piece(3), placed_row, placed_col)
    for v in range(4):
        for r in range(row_count):
            for c in range(2):
                outbox[2 * r + c, v * blocks : (v + 1) * blocks, :] = values[v][
                    r * blocks : (r + 1) * blocks, c * LANES : (c + 1) * LANES
                ]

    pl.semaphore_wait(barrier, tiles - 1)

    def sounding_copy(peer):
        return pltpu.make_async_remote_copy(
            src_ref=outbox.at[peer], dst_ref=inbox.at[me],
            send_sem=send_sem.at[peer], recv_sem=recv_sem.at[me],
            device_id={"row": peer // 2, "col": lax.rem(peer, 2)}, device_id_type=MESH,
        )

    def arrived(origin):
        pltpu.make_async_remote_copy(
            src_ref=outbox.at[origin], dst_ref=inbox.at[origin],
            send_sem=send_sem.at[origin], recv_sem=recv_sem.at[origin],
            device_id={"row": origin // 2, "col": lax.rem(origin, 2)}, device_id_type=MESH,
        ).wait_recv()

    sounding_copy(2 * my_row + other).start()

    def send(step, carry):
        peer_row = lax.rem(my_row + row_count - step, row_count)
        sounding_copy(2 * peer_row + my_col).start()
        sounding_copy(2 * peer_row + other).start()
        return carry

    lax.fori_loop(1, row_count, send, 0)

    strip = pl.ds(pl.multiple_of((1 - my_col) * (tile_cols - LANES), LANES), LANES)
    side = pl.ds(tile_cols, LANES)
    body = pl.ds(0, tile_cols)
    top, bottom = pl.ds(MARGIN, HALO), pl.ds(MARGIN + HALO + tile_rows, HALO)
    has_up, has_down = my_row > 0, my_row < row_count - 1

    def halo_copies(cut, put, sends, recvs):
        first, last = (0, HALO), (tile_rows - HALO, HALO)
        plan = (
            (has_up, -1, my_col, first, body, bottom, body),
            (has_down, 1, my_col, last, body, top, body),
            (None, 0, other, (0, tile_rows), strip, interior, side),
            (has_up, -1, other, first, strip, bottom, side),
            (has_down, 1, other, last, strip, top, side),
        )
        return [
            (
                condition,
                pltpu.make_async_remote_copy(
                    src_ref=cut(rows, columns), dst_ref=put(to_rows, to_columns),
                    send_sem=sends.at[n], recv_sem=recvs.at[n],
                    device_id={
                        "row": jnp.clip(my_row + shift, 0, row_count - 1),
                        "col": to_col,
                    },
                    device_id_type=MESH,
                ),
            )
            for n, (condition, shift, to_col, rows, columns, to_rows, to_columns) in enumerate(plan)
        ]

    def under(condition, action):
        if condition is None:
            action()
        else:
            pl.when(condition)(action)

    mirrored = (has_down, has_up, None, has_down, has_up)

    def finish(copies):
        for (condition, copy), from_there in zip(copies, mirrored):
            under(condition, copy.wait_send)
            under(from_there, copy.wait_recv)

    field_copies = halo_copies(
        lambda rows, columns: start.at[pl.ds(*rows), columns],
        lambda rows, columns: field.at[0, rows, columns],
        halo_send, halo_recv,
    )
    for condition, copy in field_copies:
        under(condition, copy.start)

    def blank(rows):
        def action():
            field[0, rows, :] = jnp.zeros((HALO, field.shape[2]), f32)
            grid[:, rows, :] = jnp.zeros((2, HALO, field.shape[2]), f32)
        return action

    pl.when(jnp.logical_not(has_up))(blank(top))
    pl.when(jnp.logical_not(has_down))(blank(bottom))
    for n in range(2):
        field[n, :MARGIN, :] = jnp.zeros((MARGIN, field.shape[2]), f32)
        field[n, MARGIN + ext_rows :, :] = jnp.zeros((MARGIN, field.shape[2]), f32)
    field[0, interior, :tile_cols] = start[...]

    row_ids = lax.broadcasted_iota(jnp.int32, (tile_rows, LANES), 0).astype(f32)
    col_ids = lax.broadcasted_iota(jnp.int32, (LANES, LANES), 0).astype(f32)
    chunks = tile_cols // LANES

    def grid_pair(source_row, first):
        for c in range(2):
            origin = 2 * source_row + c
            for b in range(blocks):
                lanes = slice((c * blocks + b) * LANES, (c * blocks + b + 1) * LANES)
                w, m, r, k = (
                    inbox[origin, v * blocks + b : v * blocks + b + 1, :] for v in range(4)
                )
                (w_high, w_low), (m_high, m_low) = two_pieces(w), two_pieces(m)
                chosen = row_ids == r
                left[:, lanes] = jnp.concatenate(
                    [jnp.where(chosen, x, 0.0) for x in (w_high, m_high, w_low, m_low)], axis=0
                ).astype(bf16)
                chunk = jnp.floor(k * (1.0 / LANES))
                base = jnp.where(col_ids == k - LANES * chunk, 1.0, 0.0).astype(bf16)
                base = base.reshape(LANES // 16, 16, LANES)
                chunk = jnp.broadcast_to(chunk, (16, LANES))
                for n in range(chunks):
                    mask = jnp.where(chunk == float(n), 1.0, 0.0).astype(bf16)
                    right[n * LANES : (n + 1) * LANES, lanes] = (base * mask[None]).reshape(
                        LANES, LANES
                    )
        term = lax.dot_general(right[...], left[...], NT, preferred_element_type=f32)
        if first:
            total[...] = term
        else:
            total[...] += term

    inbox[me] = outbox[me]
    arrived(2 * my_row + other)
    grid_pair(my_row, True)

    def grid_step(step, carry):
        source_row = lax.rem(my_row + step, row_count)
        arrived(2 * source_row)
        arrived(2 * source_row + 1)
        grid_pair(source_row, False)
        return carry

    lax.fori_loop(1, row_count, grid_step, 0)

    half = 2 * tile_rows
    for n in range(chunks):
        part = total[n * LANES : (n + 1) * LANES, :]
        both = (part[:, :half] + part[:, half:]).T
        lanes = slice(n * LANES, (n + 1) * LANES)
        scale = damping / (centre_weight + both[:tile_rows])
        grid[0, interior, lanes] = scale
        grid[1, interior, lanes] = scale * both[tile_rows:]

    grid_copies = halo_copies(
        lambda rows, columns: grid.at[:, pl.ds(MARGIN + HALO + rows[0], rows[1]), columns],
        lambda rows, columns: grid.at[:, rows, columns],
        grid_send, grid_recv,
    )
    for condition, copy in grid_copies:
        under(condition, copy.start)

    def sent(step, carry):
        peer = lax.rem(me + step, tiles)
        sounding_copy(peer).wait_send()
        return carry

    lax.fori_loop(1, tiles, sent, 0)
    finish(field_copies)
    finish(grid_copies)

    strip_lane = lax.broadcasted_iota(jnp.int32, (ext_rows, LANES), 1)
    nearer = (strip_lane < LANES // 2) == (my_col == 0)
    ext = slice(MARGIN, MARGIN + ext_rows)
    field[0, ext, tile_cols:] = jnp.where(nearer, field[0, ext, tile_cols:], 0.0)
    for n in range(2):
        grid[n, ext, tile_cols:] = jnp.where(nearer, grid[n, ext, tile_cols:], 0.0)

    width = field.shape[2]

    def relaxed(now, at):
        centre = field[now, at : at + 8, :]
        ring = field[now, at - 1 : at + 7, :] + field[now, at + 1 : at + 9, :]
        far = field[now, at - 2 : at + 6, :] + field[now, at + 2 : at + 10, :]
        beside = near_weight * centre - corner_weight * ring
        beside = pltpu.roll(beside, 1, 1) + pltpu.roll(beside, width - 1, 1)
        far = far + (pltpu.roll(centre, 2, 1) + pltpu.roll(centre, width - 2, 1))
        pull = near_weight * ring + beside - distant_weight * far
        return 0.5 * centre + (grid[1, at : at + 8, :] + grid[0, at : at + 8, :] * pull)

    def sweep(level, carry):
        now = lax.rem(level, 2)
        for at in range(MARGIN, MARGIN + ext_rows, 8):
            field[1 - now, at : at + 8, :] = relaxed(now, at)
        return carry

    lax.fori_loop(0, SWEEPS - 1, sweep, 0)
    for at in range(MARGIN + HALO, MARGIN + HALO + tile_rows, 8):
        new = relaxed((SWEEPS - 1) % 2, at)
        out[at - MARGIN - HALO : at - MARGIN - HALO + 8, :] = new[:, :tile_cols]


def body(
    start, dest_tile, cell_row, cell_col, source_type, sounding_value, sounding_weight, type_gain
):
    tile_rows, tile_cols = start.shape
    row_count = lax.axis_size("row")
    assert lax.axis_size("col") == 2
    assert tile_rows == 64 and tile_cols <= 2048 and tile_cols % LANES == 0
    count = dest_tile.shape[0]
    assert count % (8 * LANES) == 0
    sounding_rows = count // LANES
    tiles = 2 * row_count
    capacity = 5 * count // (4 * tiles)
    blocks = -(-capacity // LANES)
    box_rows = -(-4 * blocks // 8) * 8
    slot_rows = row_count * blocks
    width = tile_cols + LANES
    tall = tile_rows + 2 * HALO + 2 * MARGIN
    depth = 2 * blocks * LANES
    vmem = pl.BlockSpec(memory_space=pltpu.VMEM)
    call = pl.pallas_call(
        functools.partial(kernel, row_count, blocks),
        out_shape=jax.ShapeDtypeStruct(start.shape, f32),
        in_specs=[vmem] * 7 + [pl.BlockSpec(memory_space=pltpu.SMEM)],
        out_specs=vmem,
        scratch_shapes=[
            pltpu.VMEM((tiles, box_rows, LANES), f32),
            pltpu.VMEM((tiles, box_rows, LANES), f32),
            pltpu.VMEM((6 * slot_rows, 8 * LANES), bf16),
            pltpu.VMEM((2 * LANES, 8 * LANES), bf16),
            pltpu.VMEM((6 * slot_rows, 2 * LANES), f32),
            pltpu.VMEM((2, sounding_rows, LANES), jnp.int32),
            pltpu.VMEM((6, sounding_rows, LANES), f32),
            pltpu.VMEM((4 * tile_rows, depth), bf16),
            pltpu.VMEM((tile_cols, depth), bf16),
            pltpu.VMEM((tile_cols, 4 * tile_rows), f32),
            pltpu.VMEM((2, tall, width), f32),
            pltpu.VMEM((2, tall, width), f32),
            pltpu.SemaphoreType.DMA((tiles,)),
            pltpu.SemaphoreType.DMA((tiles,)),
            pltpu.SemaphoreType.DMA((5,)),
            pltpu.SemaphoreType.DMA((5,)),
            pltpu.SemaphoreType.DMA((5,)),
            pltpu.SemaphoreType.DMA((5,)),
        ],
        compiler_params=pltpu.CompilerParams(
            collective_id=0, has_side_effects=True, vmem_limit_bytes=48 * 1024 * 1024
        ),
    )
    shaped = (sounding_rows, LANES)
    return call(
        start, dest_tile.reshape(shaped), cell_row.reshape(shaped), cell_col.reshape(shaped),
        source_type.reshape(shaped), sounding_value.reshape(shaped),
        sounding_weight.reshape(shaped), type_gain,
    )


def solution(mesh):
    many = P(("slab", "row", "col"))
    in_specs = (P(("slab", "row"), "col"), many, many, many, many, many, many, P())
    out_specs = P(("slab", "row"), "col")
    return jax.shard_map(body, mesh=mesh, in_specs=in_specs, out_specs=out_specs, check_vma=False)
```

time: 171 us -> 44.2 us (0.26)
  matrix products: 72.3 us -> 0 us
  starting transfers between devices: 46 us -> 0 us
  Pallas kernels: 0 us -> 36.6 us
  other arithmetic: 21.7 us -> 0 us
  waiting for transfers between devices: 16 us -> 0 us
  local copies, waits for them, and re-layouts: 12.4 us -> 7.04 us
    dot_general x37 -> x0, matrix products: 72.3 us -> none  [the longest x5 34.6 us: grid_block(): lax.dot_general(left, col_onehot, (((0,), (0,)), ((), ())), precision=lax...]
    ppermute x16 -> x0, starting transfers between devices: 39 us -> none  [the longest x8 23.5 us: padded_2(): after = lax.ppermute(leading, axis, down)]
    pallas_call x0 -> x1, Pallas kernels: none -> 36.6 us  [body(): call(start, dest_tile.reshape(shaped), cell_row.reshape(shaped), cell_col...]
    ppermute x16 -> x0, waiting for transfers between devices: 15.2 us -> none  [the longest x8 15.2 us: padded_2(): before = lax.ppermute(last, axis, up)]
    slice x10 -> x0, local copies, waits for them, and re-layouts: 7.25 us -> none  [the longest x5 4.88 us: grid_block(): block[0][:, None]]
    mul x6 -> x0, other arithmetic: 7.1 us -> none  [the longest x5 4.37 us: grid_block(): row_onehot * block[0][:, None]]
    all_to_all x1 -> x0, starting transfers between devices: 7.03 us -> none  [body(): lax.all_to_all(outgoing, ('row', 'col'), split_axis=1, concat_axis=1, til...]
    unnamed x3 -> x17, local copies, waits for them, and re-layouts: 0.04 us -> 7.04 us
  transfers between devices with their start and end apart: 17 -> 0, of which waited for: 8 -> 0; matrix products, arithmetic and copies ran while one was open for 31% -> 0% of each run, Pallas kernels for 0% -> 0%
where the time goes in v1:
time: 44.2 us; the launch traced here: 43.6 us
  Pallas kernels  36.6 us (83%)
  local copies, waits for them, and re-layouts  7.04 us (16%)
    pallas_call x1, Pallas kernels, body(): call(start, dest_tile.reshape(shaped), cell_row.reshape(shaped), cell_col...  36.6 us
    unnamed x17, local copies, waits for them, and re-layouts  7.04 us

profile of v1, /device:TPU:13, one launch (start us, length us, event | category | flops | bytes accessed | tf_op | source)
XLA Modules:
  0.0 43.6 jit_solution(5878276947062560328)
XLA Ops:
  0.0 0.0 copy-start.7
  0.0 0.7 %copy-done.7 = f32[3]{0:T(128)S(1)} copy-done((f32[3]{0:T(128)S(1)}, f32[3]{0:T(128)}, u32[]{:S(2)}) %copy-start.7) | copy-done | bytes 36
  0.7 0.0 copy-start
  0.7 1.0 %copy-done = f32[64,2048]{1,0:T(8,128)S(1)} copy-done((f32[64,2048]{1,0:T(8,128)S(1)}, f32[64,2048]{1,0:T(8,128)}, u32[]{:S(2)}) %copy-start) | copy-done | bytes 524312
  1.7 0.0 copy-start.1
  1.7 0.8 %copy-done.1 = s32[8192]{0:T(1024)S(1)} copy-done((s32[8192]{0:T(1024)S(1)}, s32[8192]{0:T(1024)}, u32[]{:S(2)}) %copy-start.1) | copy-done | bytes 32792
  2.5 0.0 copy-start.2
  2.5 0.8 %copy-done.2 = s32[8192]{0:T(1024)S(1)} copy-done((s32[8192]{0:T(1024)S(1)}, s32[8192]{0:T(1024)}, u32[]{:S(2)}) %copy-start.2) | copy-done | bytes 32792
  3.2 0.0 copy-start.3
  3.2 0.8 %copy-done.3 = s32[8192]{0:T(1024)S(1)} copy-done((s32[8192]{0:T(1024)S(1)}, s32[8192]{0:T(1024)}, u32[]{:S(2)}) %copy-start.3) | copy-done | bytes 32792
  4.0 0.0 copy-start.4
  4.0 0.8 %copy-done.4 = s32[8192]{0:T(1024)S(1)} copy-done((s32[8192]{0:T(1024)S(1)}, s32[8192]{0:T(1024)}, u32[]{:S(2)}) %copy-start.4) | copy-done | bytes 32792
  4.7 0.0 copy-start.5
  4.7 0.8 %copy-done.5 = f32[8192]{0:T(1024)S(1)} copy-done((f32[8192]{0:T(1024)S(1)}, f32[8192]{0:T(1024)}, u32[]{:S(2)}) %copy-start.5) | copy-done | bytes 32792
  5.5 0.0 copy-start.6
  5.5 0.8 %copy-done.6 = f32[8192]{0:T(1024)S(1)} copy-done((f32[8192]{0:T(1024)S(1)}, f32[8192]{0:T(1024)}, u32[]{:S(2)}) %copy-start.6) | copy-done | bytes 32792
  6.2 36.6 %shard_map.82 = f32[64,2048]{1,0:T(8,128)S(1)} custom-call(f32[64,2048]{1,0:T(8,128)S(1)} %copy-done, s32[64,128]{1,0:T(8,128)S(1)} %bitcast.6, s32[64,128]{1,0:T(8,128)S(1)} %bitcast.7, s32[64,128]{1,0:T(8,128)S(1)} %bitcast.8, s32[64,128]{1,0:T(8,128)S(1)} %bitcast.9, f32[64,128]{1,0:T(8,128)S(1)} %bitcast.10, f32[64,128]{1,0:T(8,128)S(1)} %bitcast.11, ...), custom_call_target="tpu_custom_call" | custom-call | tf_op jit(solution)/shard_map/pallas_call | solution.py:373
  42.8 0.8 %copy.10 = f32[64,2048]{1,0:T(8,128)} copy(f32[64,2048]{1,0:T(8,128)S(1)} %shard_map.82) | data formatting | bytes 1048576
Async XLA Ops:
  0.0 0.7 %copy-start.7 = (f32[3]{0:T(128)S(1)}, f32[3]{0:T(128)}, u32[]{:S(2)}) copy-start(f32[3]{0:T(128)} %gain.1) | copy-start | bytes 40
  0.7 1.0 %copy-start = (f32[64,2048]{1,0:T(8,128)S(1)}, f32[64,2048]{1,0:T(8,128)}, u32[]{:S(2)}) copy-start(f32[64,2048]{1,0:T(8,128)} %start.1) | copy-start | bytes 1572868
  1.7 0.8 %copy-start.1 = (s32[8192]{0:T(1024)S(1)}, s32[8192]{0:T(1024)}, u32[]{:S(2)}) copy-start(s32[8192]{0:T(1024)} %param.9) | copy-start | bytes 98308
  2.5 0.8 %copy-start.2 = (s32[8192]{0:T(1024)S(1)}, s32[8192]{0:T(1024)}, u32[]{:S(2)}) copy-start(s32[8192]{0:T(1024)} %param.10) | copy-start | bytes 98308
  3.2 0.8 %copy-start.3 = (s32[8192]{0:T(1024)S(1)}, s32[8192]{0:T(1024)}, u32[]{:S(2)}) copy-start(s32[8192]{0:T(1024)} %param.11) | copy-start | bytes 98308
  4.0 0.8 %copy-start.4 = (s32[8192]{0:T(1024)S(1)}, s32[8192]{0:T(1024)}, u32[]{:S(2)}) copy-start(s32[8192]{0:T(1024)} %param.12) | copy-start | bytes 98308
  4.7 0.8 %copy-start.5 = (f32[8192]{0:T(1024)S(1)}, f32[8192]{0:T(1024)}, u32[]{:S(2)}) copy-start(f32[8192]{0:T(1024)} %param.13) | copy-start | bytes 98308
  5.5 0.8 %copy-start.6 = (f32[8192]{0:T(1024)S(1)}, f32[8192]{0:T(1024)}, u32[]{:S(2)}) copy-start(f32[8192]{0:T(1024)} %param.14) | copy-start | bytes 98308

commit v2 on v1

--- a/solution.py
+++ b/solution.py
@@ -30,11 +30,16 @@
     return high, x - high
 
 
-def kernel(
-    row_count, blocks, start, dest, cell_row, cell_col, source, value, weight, gain, out,
-    outbox, inbox, left_route, right_route, routed, slots, pieces, left, right, total,
-    field, grid, send_sem, recv_sem, halo_send, halo_recv, grid_send, grid_recv,
-):
+def kernel(row_count, blocks, start, *refs):
+    soundings, gain_in, out = refs[:6], refs[6], refs[7]
+    whole_numbers, reals, gain, load_sem = refs[8:12]
+    dest, cell_row, cell_col, source = (whole_numbers.at[n] for n in range(4))
+    value, weight = (reals.at[n] for n in range(2))
+    (
+        outbox, inbox, left_route, right_route, routed, slots, pieces,
+        left, right, total, field, grid, send_sem,
+        recv_sem, halo_send, halo_recv, grid_send, grid_recv,
+    ) = refs[12:]
     tile_rows, tile_cols = start.shape
     sounding_rows = dest.shape[0]
     tiles = 2 * row_count
@@ -44,6 +49,20 @@
     ext_rows = tile_rows + 2 * HALO
     interior = pl.ds(MARGIN + HALO, tile_rows)
 
+    loads = [
+        pltpu.make_async_copy(array, place, load_sem.at[n])
+        for n, (array, place) in enumerate(
+            zip(soundings, (dest, cell_row, cell_col, source, value, weight))
+        )
+    ]
+    loads.append(pltpu.make_async_copy(gain_in, gain, load_sem.at[6]))
+    start_load = pltpu.make_async_copy(
+        start, field.at[0, interior, pl.ds(0, tile_cols)], load_sem.at[7]
+    )
+    for load in loads:
+        load.start()
+    start_load.start()
+
     barrier = pltpu.get_barrier_semaphore()
 
     def greet(step, carry):
@@ -56,6 +75,8 @@
 
     lax.fori_loop(1, tiles, greet, 0)
 
+    for load in loads:
+        load.wait()
     destination = dest[...]
     lane_a = lax.broadcasted_iota(jnp.int32, (LANES, 2 * LANES), 0)
     lane_b = lax.broadcasted_iota(jnp.int32, (LANES, 2 * LANES), 1)
@@ -193,8 +214,9 @@
 
     mirrored = (has_down, has_up, None, has_down, has_up)
 
-    def finish(copies):
-        for (condition, copy), from_there in zip(copies, mirrored):
+    def finish(copies, which=range(5)):
+        for (condition, copy), n in zip(copies, which):
+            from_there = mirrored[n]
             under(condition, copy.wait_send)
             under(from_there, copy.wait_recv)
 
@@ -214,10 +236,10 @@
 
     pl.when(jnp.logical_not(has_up))(blank(top))
     pl.when(jnp.logical_not(has_down))(blank(bottom))
-    for n in range(2):
+    for n in range(SWEEPS):
         field[n, :MARGIN, :] = jnp.zeros((MARGIN, field.shape[2]), f32)
         field[n, MARGIN + ext_rows :, :] = jnp.zeros((MARGIN, field.shape[2]), f32)
-    field[0, interior, :tile_cols] = start[...]
+    start_load.wait()
 
     row_ids = lax.broadcasted_iota(jnp.int32, (tile_rows, LANES), 0).astype(f32)
     col_ids = lax.broadcasted_iota(jnp.int32, (LANES, LANES), 0).astype(f32)
@@ -278,8 +300,8 @@
         lambda rows, columns: grid.at[:, rows, columns],
         grid_send, grid_recv,
     )
-    for condition, copy in grid_copies:
-        under(condition, copy.start)
+    for n in (2, 0, 1, 3, 4):
+        under(grid_copies[n][0], grid_copies[n][1].start)
 
     def sent(step, carry):
         peer = lax.rem(me + step, tiles)
@@ -288,14 +310,17 @@
 
     lax.fori_loop(1, tiles, sent, 0)
     finish(field_copies)
-    finish(grid_copies)
-
-    strip_lane = lax.broadcasted_iota(jnp.int32, (ext_rows, LANES), 1)
-    nearer = (strip_lane < LANES // 2) == (my_col == 0)
-    ext = slice(MARGIN, MARGIN + ext_rows)
-    field[0, ext, tile_cols:] = jnp.where(nearer, field[0, ext, tile_cols:], 0.0)
+    grid_copies[2][1].wait()
+
+    def keep_nearer(ref, rows, n):
+        strip_lane = lax.broadcasted_iota(jnp.int32, (rows.stop - rows.start, LANES), 1)
+        nearer = (strip_lane < LANES // 2) == (my_col == 0)
+        ref[n, rows, tile_cols:] = jnp.where(nearer, ref[n, rows, tile_cols:], 0.0)
+
+    first_row, last_row = MARGIN + HALO, MARGIN + HALO + tile_rows
+    keep_nearer(field, slice(MARGIN, MARGIN + ext_rows), 0)
     for n in range(2):
-        grid[n, ext, tile_cols:] = jnp.where(nearer, grid[n, ext, tile_cols:], 0.0)
+        keep_nearer(grid, slice(first_row, last_row), n)
 
     width = field.shape[2]
 
@@ -309,16 +334,36 @@
         pull = near_weight * ring + beside - distant_weight * far
         return 0.5 * centre + (grid[1, at : at + 8, :] + grid[0, at : at + 8, :] * pull)
 
-    def sweep(level, carry):
-        now = lax.rem(level, 2)
-        for at in range(MARGIN, MARGIN + ext_rows, 8):
-            field[1 - now, at : at + 8, :] = relaxed(now, at)
-        return carry
-
-    lax.fori_loop(0, SWEEPS - 1, sweep, 0)
-    for at in range(MARGIN + HALO, MARGIN + HALO + tile_rows, 8):
-        new = relaxed((SWEEPS - 1) % 2, at)
-        out[at - MARGIN - HALO : at - MARGIN - HALO + 8, :] = new[:, :tile_cols]
+    def update(level, rows):
+        for at in rows:
+            field[level + 1, at : at + 8, :] = relaxed(level, at)
+
+    def finished(rows):
+        for at in rows:
+            new = relaxed(SWEEPS - 1, at)
+            out[at - first_row : at - first_row + 8, :] = new[:, :tile_cols]
+
+    def inner(level, carry):
+        update(level, range(first_row, last_row, 8))
+        return carry
+
+    lax.fori_loop(0, SWEEPS - 1, inner, 0)
+    finished(range(first_row + 8, last_row - 8, 8))
+
+    finish([(c, k) for n, (c, k) in enumerate(grid_copies) if n != 2], (0, 1, 3, 4))
+    for rows in (slice(MARGIN, first_row), slice(last_row, last_row + HALO)):
+        for n in range(2):
+            keep_nearer(grid, rows, n)
+    edges = (first_row - 8, last_row)
+    ends = (first_row, last_row - 8)
+    update(0, edges)
+
+    def outer(level, carry):
+        update(level, edges + ends)
+        return carry
+
+    lax.fori_loop(1, SWEEPS - 1, outer, 0)
+    finished(ends)
 
 
 def body(
@@ -343,9 +388,13 @@
     call = pl.pallas_call(
         functools.partial(kernel, row_count, blocks),
         out_shape=jax.ShapeDtypeStruct(start.shape, f32),
-        in_specs=[vmem] * 7 + [pl.BlockSpec(memory_space=pltpu.SMEM)],
+        in_specs=[pl.BlockSpec(memory_space=pltpu.HBM)] * 8,
         out_specs=vmem,
         scratch_shapes=[
+            pltpu.VMEM((4, sounding_rows, LANES), jnp.int32),
+            pltpu.VMEM((2, sounding_rows, LANES), f32),
+            pltpu.SMEM((3,), f32),
+            pltpu.SemaphoreType.DMA((8,)),
             pltpu.VMEM((tiles, box_rows, LANES), f32),
             pltpu.VMEM((tiles, box_rows, LANES), f32),
             pltpu.VMEM((6 * slot_rows, 8 * LANES), bf16),
@@ -356,7 +405,7 @@
             pltpu.VMEM((4 * tile_rows, depth), bf16),
             pltpu.VMEM((tile_cols, depth), bf16),
             pltpu.VMEM((tile_cols, 4 * tile_rows), f32),
-            pltpu.VMEM((2, tall, width), f32),
+            pltpu.VMEM((SWEEPS, tall, width), f32),
             pltpu.VMEM((2, tall, width), f32),
             pltpu.SemaphoreType.DMA((tiles,)),
             pltpu.SemaphoreType.DMA((tiles,)),

time: 44.2 us -> 40.2 us (0.910)
  Pallas kernels: 36.6 us -> 32.5 us
    pallas_call x1, Pallas kernels: 36.6 us -> 32.5 us  [body(): call(start, dest_tile.reshape(shaped), cell_row.reshape(shaped), cell_col...]
where the time goes in v2:
time: 40.2 us; the launch traced here: 39.6 us
  Pallas kernels  32.5 us (81%)
  local copies, waits for them, and re-layouts  7.04 us (18%)
    pallas_call x1, Pallas kernels, body(): call(start, dest_tile.reshape(shaped), cell_row.reshape(shaped), cell_col...  32.5 us
    unnamed x17, local copies, waits for them, and re-layouts  7.04 us

profile of v2, /device:TPU:13, one launch (start us, length us, event | category | flops | bytes accessed | tf_op | source)
XLA Modules:
  0.0 39.6 jit_solution(11024034484742703211)
XLA Ops:
  0.0 0.0 copy-start.7
  0.0 0.7 %copy-done.7 = f32[3]{0:T(128)S(1)} copy-done((f32[3]{0:T(128)S(1)}, f32[3]{0:T(128)}, u32[]{:S(2)}) %copy-start.7) | copy-done | bytes 36
  0.7 0.0 copy-start
  0.7 1.0 %copy-done = f32[64,2048]{1,0:T(8,128)S(1)} copy-done((f32[64,2048]{1,0:T(8,128)S(1)}, f32[64,2048]{1,0:T(8,128)}, u32[]{:S(2)}) %copy-start) | copy-done | bytes 524312
  1.7 0.0 copy-start.1
  1.7 0.8 %copy-done.1 = s32[8192]{0:T(1024)S(1)} copy-done((s32[8192]{0:T(1024)S(1)}, s32[8192]{0:T(1024)}, u32[]{:S(2)}) %copy-start.1) | copy-done | bytes 32792
  2.5 0.0 copy-start.2
  2.5 0.8 %copy-done.2 = s32[8192]{0:T(1024)S(1)} copy-done((s32[8192]{0:T(1024)S(1)}, s32[8192]{0:T(1024)}, u32[]{:S(2)}) %copy-start.2) | copy-done | bytes 32792
  3.2 0.0 copy-start.3
  3.2 0.8 %copy-done.3 = s32[8192]{0:T(1024)S(1)} copy-done((s32[8192]{0:T(1024)S(1)}, s32[8192]{0:T(1024)}, u32[]{:S(2)}) %copy-start.3) | copy-done | bytes 32792
  4.0 0.0 copy-start.4
  4.0 0.8 %copy-done.4 = s32[8192]{0:T(1024)S(1)} copy-done((s32[8192]{0:T(1024)S(1)}, s32[8192]{0:T(1024)}, u32[]{:S(2)}) %copy-start.4) | copy-done | bytes 32792
  4.7 0.0 copy-start.5
  4.7 0.8 %copy-done.5 = f32[8192]{0:T(1024)S(1)} copy-done((f32[8192]{0:T(1024)S(1)}, f32[8192]{0:T(1024)}, u32[]{:S(2)}) %copy-start.5) | copy-done | bytes 32792
  5.5 0.0 copy-start.6
  5.5 0.8 %copy-done.6 = f32[8192]{0:T(1024)S(1)} copy-done((f32[8192]{0:T(1024)S(1)}, f32[8192]{0:T(1024)}, u32[]{:S(2)}) %copy-start.6) | copy-done | bytes 32792
  6.2 32.5 %shard_map.82 = f32[64,2048]{1,0:T(8,128)S(1)} custom-call(f32[64,2048]{1,0:T(8,128)S(1)} %copy-done, s32[64,128]{1,0:T(8,128)S(1)} %bitcast.6, s32[64,128]{1,0:T(8,128)S(1)} %bitcast.7, s32[64,128]{1,0:T(8,128)S(1)} %bitcast.8, s32[64,128]{1,0:T(8,128)S(1)} %bitcast.9, f32[64,128]{1,0:T(8,128)S(1)} %bitcast.10, f32[64,128]{1,0:T(8,128)S(1)} %bitcast.11, ...), custom_call_target="tpu_custom_call" | custom-call | tf_op jit(solution)/shard_map/pallas_call | solution.py:422
  38.8 0.8 %copy.10 = f32[64,2048]{1,0:T(8,128)} copy(f32[64,2048]{1,0:T(8,128)S(1)} %shard_map.82) | data formatting | bytes 1048576
Async XLA Ops:
  0.0 0.7 %copy-start.7 = (f32[3]{0:T(128)S(1)}, f32[3]{0:T(128)}, u32[]{:S(2)}) copy-start(f32[3]{0:T(128)} %refs_6_.1) | copy-start | bytes 40
  0.7 1.0 %copy-start = (f32[64,2048]{1,0:T(8,128)S(1)}, f32[64,2048]{1,0:T(8,128)}, u32[]{:S(2)}) copy-start(f32[64,2048]{1,0:T(8,128)} %start.1) | copy-start | bytes 1572868
  1.7 0.8 %copy-start.1 = (s32[8192]{0:T(1024)S(1)}, s32[8192]{0:T(1024)}, u32[]{:S(2)}) copy-start(s32[8192]{0:T(1024)} %param.9) | copy-start | bytes 98308
  2.5 0.8 %copy-start.2 = (s32[8192]{0:T(1024)S(1)}, s32[8192]{0:T(1024)}, u32[]{:S(2)}) copy-start(s32[8192]{0:T(1024)} %param.10) | copy-start | bytes 98308
  3.2 0.8 %copy-start.3 = (s32[8192]{0:T(1024)S(1)}, s32[8192]{0:T(1024)}, u32[]{:S(2)}) copy-start(s32[8192]{0:T(1024)} %param.11) | copy-start | bytes 98308
  4.0 0.8 %copy-start.4 = (s32[8192]{0:T(1024)S(1)}, s32[8192]{0:T(1024)}, u32[]{:S(2)}) copy-start(s32[8192]{0:T(1024)} %param.12) | copy-start | bytes 98308
  4.7 0.8 %copy-start.5 = (f32[8192]{0:T(1024)S(1)}, f32[8192]{0:T(1024)}, u32[]{:S(2)}) copy-start(f32[8192]{0:T(1024)} %param.13) | copy-start | bytes 98308
  5.5 0.8 %copy-start.6 = (f32[8192]{0:T(1024)S(1)}, f32[8192]{0:T(1024)}, u32[]{:S(2)}) copy-start(f32[8192]{0:T(1024)} %param.14) | copy-start | bytes 98308

commit v3 on v2

--- a/solution.py
+++ b/solution.py
@@ -8,6 +8,8 @@
 from jax.sharding import PartitionSpec as P
 
 SWEEPS = 4
+PARTS = 4
+LATE = 4
 LANES = 128
 HALO = 2 * SWEEPS
 MARGIN = 8
@@ -37,8 +39,8 @@
     value, weight = (reals.at[n] for n in range(2))
     (
         outbox, inbox, left_route, right_route, routed, slots, pieces,
-        left, right, total, field, grid, send_sem,
-        recv_sem, halo_send, halo_recv, grid_send, grid_recv,
+        left, base, chunk_of, right, right_late, total, field, grid, send_sem,
+        recv_sem, halo_send, halo_recv, grid_send, grid_recv, row_send, row_recv,
     ) = refs[12:]
     tile_rows, tile_cols = start.shape
     sounding_rows = dest.shape[0]
@@ -245,7 +247,11 @@
     col_ids = lax.broadcasted_iota(jnp.int32, (LANES, LANES), 0).astype(f32)
     chunks = tile_cols // LANES
 
-    def grid_pair(source_row, first):
+    late = left.shape[0]
+    span = tile_cols // PARTS
+    span_chunks = span // LANES
+
+    def prepare(source_row, slot):
         for c in range(2):
             origin = 2 * source_row + c
             for b in range(blocks):
@@ -255,20 +261,33 @@
                 )
                 (w_high, w_low), (m_high, m_low) = two_pieces(w), two_pieces(m)
                 chosen = row_ids == r
-                left[:, lanes] = jnp.concatenate(
+                left[slot, :, lanes] = jnp.concatenate(
                     [jnp.where(chosen, x, 0.0) for x in (w_high, m_high, w_low, m_low)], axis=0
                 ).astype(bf16)
                 chunk = jnp.floor(k * (1.0 / LANES))
-                base = jnp.where(col_ids == k - LANES * chunk, 1.0, 0.0).astype(bf16)
-                base = base.reshape(LANES // 16, 16, LANES)
-                chunk = jnp.broadcast_to(chunk, (16, LANES))
-                for n in range(chunks):
-                    mask = jnp.where(chunk == float(n), 1.0, 0.0).astype(bf16)
-                    right[n * LANES : (n + 1) * LANES, lanes] = (base * mask[None]).reshape(
-                        LANES, LANES
-                    )
-        term = lax.dot_general(right[...], left[...], NT, preferred_element_type=f32)
-        if first:
+                base[slot, :, lanes] = jnp.where(
+                    col_ids == k - LANES * chunk, 1.0, 0.0
+                ).astype(bf16)
+                chunk_of[slot, :, lanes] = jnp.broadcast_to(chunk, (8, LANES))
+
+    def spread(target, slot, offset, first_chunk, count):
+        for b in range(2 * blocks):
+            lanes = slice(b * LANES, (b + 1) * LANES)
+            to = slice(offset + b * LANES, offset + (b + 1) * LANES)
+            shared = base[slot, :, lanes].reshape(LANES // 16, 16, LANES)
+            chunk = chunk_of[slot, :, lanes]
+            chunk = jnp.concatenate([chunk, chunk], axis=0)
+            for n in range(count):
+                mask = jnp.where(chunk == first_chunk + float(n), 1.0, 0.0).astype(bf16)
+                target[n * LANES : (n + 1) * LANES, to] = (shared * mask[None]).reshape(
+                    LANES, LANES
+                )
+
+    def grid_pair(source_row, begin):
+        prepare(source_row, 0)
+        spread(right, 0, 0, 0.0, chunks)
+        term = lax.dot_general(right[...], left[0], NT, preferred_element_type=f32)
+        if begin:
             total[...] = term
         else:
             total[...] += term
@@ -284,24 +303,77 @@
         grid_pair(source_row, False)
         return carry
 
-    lax.fori_loop(1, row_count, grid_step, 0)
-
-    half = 2 * tile_rows
-    for n in range(chunks):
-        part = total[n * LANES : (n + 1) * LANES, :]
-        both = (part[:, :half] + part[:, half:]).T
-        lanes = slice(n * LANES, (n + 1) * LANES)
-        scale = damping / (centre_weight + both[:tile_rows])
-        grid[0, interior, lanes] = scale
-        grid[1, interior, lanes] = scale * both[tile_rows:]
+    lax.fori_loop(1, row_count - late, grid_step, 0)
+
+    def late_step(slot, carry):
+        source_row = lax.rem(my_row + row_count - late + slot, row_count)
+        arrived(2 * source_row)
+        arrived(2 * source_row + 1)
+        prepare(source_row, slot)
+        return carry
+
+    lax.fori_loop(0, late, late_step, 0)
 
     grid_copies = halo_copies(
         lambda rows, columns: grid.at[:, pl.ds(MARGIN + HALO + rows[0], rows[1]), columns],
         lambda rows, columns: grid.at[:, rows, columns],
         grid_send, grid_recv,
     )
-    for n in (2, 0, 1, 3, 4):
-        under(grid_copies[n][0], grid_copies[n][1].start)
+    beside_copies = grid_copies[2:]
+
+    def row_copies(part):
+        columns = pl.ds(pl.multiple_of(part * span, LANES), span)
+        plan = (
+            (has_up, -1, pl.ds(MARGIN + HALO, HALO), bottom),
+            (has_down, 1, pl.ds(MARGIN + tile_rows, HALO), top),
+        )
+        return [
+            (
+                condition,
+                pltpu.make_async_remote_copy(
+                    src_ref=grid.at[:, rows, columns], dst_ref=grid.at[:, to_rows, columns],
+                    send_sem=row_send.at[n, part], recv_sem=row_recv.at[n, part],
+                    device_id={
+                        "row": jnp.clip(my_row + shift, 0, row_count - 1), "col": my_col
+                    },
+                    device_id_type=MESH,
+                ),
+            )
+            for n, (condition, shift, rows, to_rows) in enumerate(plan)
+        ]
+
+    half = 2 * tile_rows
+    depth = left.shape[2]
+
+    def part_step(step, carry):
+        part = step + (1 - my_col) * (PARTS - 1 - 2 * step)
+        first_chunk = (part * span_chunks).astype(f32)
+        term = total[pl.ds(pl.multiple_of(part * span, LANES), span), :]
+        for slot in range(late):
+            spread(right_late, slot, slot * depth, first_chunk, span_chunks)
+        for slot in range(late):
+            term = term + lax.dot_general(
+                right_late[:, slot * depth : (slot + 1) * depth], left[slot], NT,
+                preferred_element_type=f32,
+            )
+        for n in range(span_chunks):
+            piece = term[n * LANES : (n + 1) * LANES]
+            both = (piece[:, :half] + piece[:, half:]).T
+            lanes = pl.ds(pl.multiple_of(part * span + n * LANES, LANES), LANES)
+            scale = damping / (centre_weight + both[:tile_rows])
+            grid[0, interior, lanes] = scale
+            grid[1, interior, lanes] = scale * both[tile_rows:]
+
+        @pl.when(step == 0)
+        def _():
+            for condition, copy in beside_copies:
+                under(condition, copy.start)
+
+        for condition, copy in row_copies(part):
+            under(condition, copy.start)
+        return carry
+
+    lax.fori_loop(0, PARTS, part_step, 0)
 
     def sent(step, carry):
         peer = lax.rem(me + step, tiles)
@@ -350,7 +422,13 @@
     lax.fori_loop(0, SWEEPS - 1, inner, 0)
     finished(range(first_row + 8, last_row - 8, 8))
 
-    finish([(c, k) for n, (c, k) in enumerate(grid_copies) if n != 2], (0, 1, 3, 4))
+    finish(beside_copies[1:], (3, 4))
+
+    def rows_done(part, carry):
+        finish(row_copies(part))
+        return carry
+
+    lax.fori_loop(0, PARTS, rows_done, 0)
     for rows in (slice(MARGIN, first_row), slice(last_row, last_row + HALO)):
         for n in range(2):
             keep_nearer(grid, rows, n)
@@ -372,7 +450,7 @@
     tile_rows, tile_cols = start.shape
     row_count = lax.axis_size("row")
     assert lax.axis_size("col") == 2
-    assert tile_rows == 64 and tile_cols <= 2048 and tile_cols % LANES == 0
+    assert tile_rows == 64 and tile_cols <= 2048 and tile_cols % (PARTS * LANES) == 0
     count = dest_tile.shape[0]
     assert count % (8 * LANES) == 0
     sounding_rows = count // LANES
@@ -384,6 +462,7 @@
     width = tile_cols + LANES
     tall = tile_rows + 2 * HALO + 2 * MARGIN
     depth = 2 * blocks * LANES
+    late = min(LATE, row_count // 2)
     vmem = pl.BlockSpec(memory_space=pltpu.VMEM)
     call = pl.pallas_call(
         functools.partial(kernel, row_count, blocks),
@@ -402,8 +481,11 @@
             pltpu.VMEM((6 * slot_rows, 2 * LANES), f32),
             pltpu.VMEM((2, sounding_rows, LANES), jnp.int32),
             pltpu.VMEM((6, sounding_rows, LANES), f32),
-            pltpu.VMEM((4 * tile_rows, depth), bf16),
+            pltpu.VMEM((late, 4 * tile_rows, depth), bf16),
+            pltpu.VMEM((late, LANES, depth), bf16),
+            pltpu.VMEM((late, 8, depth), f32),
             pltpu.VMEM((tile_cols, depth), bf16),
+            pltpu.VMEM((tile_cols // PARTS, late * depth), bf16),
             pltpu.VMEM((tile_cols, 4 * tile_rows), f32),
             pltpu.VMEM((SWEEPS, tall, width), f32),
             pltpu.VMEM((2, tall, width), f32),
@@ -413,9 +495,12 @@
             pltpu.SemaphoreType.DMA((5,)),
             pltpu.SemaphoreType.DMA((5,)),
             pltpu.SemaphoreType.DMA((5,)),
+            pltpu.SemaphoreType.DMA((2, PARTS)),
+            pltpu.SemaphoreType.DMA((2, PARTS)),
         ],
         compiler_params=pltpu.CompilerParams(
-            collective_id=0, has_side_effects=True, vmem_limit_bytes=48 * 1024 * 1024
+            collective_id=0, has_side_effects=True,
+            vmem_limit_bytes=63 * 1024 * 1024
         ),
     )
     shaped = (sounding_rows, LANES)

time: 40.2 us -> 32.6 us (0.81)
  the two profiles are of different devices: /device:TPU:13 before, /device:TPU:0 now
where the time goes in v3:
time: 32.6 us; the launch traced here: 32.5 us
  Pallas kernels  30.6 us (94%)
  local copies, waits for them, and re-layouts  1.87 us (6%)
    pallas_call x1, Pallas kernels, body(): call(start, dest_tile.reshape(shaped), cell_row.reshape(shaped), cell_col...  30.6 us
    unnamed x1, local copies, waits for them, and re-layouts  1.87 us

profile of v3, /device:TPU:0, one launch (start us, length us, event | category | flops | bytes accessed | tf_op | source)
XLA Modules:
  0.0 32.5 jit_solution(16922486747432410750)
XLA Ops:
  0.0 30.6 %shard_map.82 = f32[64,2048]{1,0:T(8,128)} custom-call(f32[64,2048]{1,0:T(8,128)} %start.1, s32[64,128]{1,0:T(8,128)} %bitcast.6, s32[64,128]{1,0:T(8,128)} %bitcast.7, s32[64,128]{1,0:T(8,128)} %bitcast.8, s32[64,128]{1,0:T(8,128)} %bitcast.9, f32[64,128]{1,0:T(8,128)} %bitcast.10, f32[64,128]{1,0:T(8,128)} %bitcast.11, f32[3]{0:T(128)} %refs_6_.1), custom_call_target="tpu_custom_call" | custom-call | tf_op jit(solution)/shard_map/pallas_call | solution.py:507
  30.6 1.9 %copy.10 = f32[64,2048]{1,0:T(8,128)} copy(f32[64,2048]{1,0:T(8,128)} %shard_map.82) | data formatting | bytes 1048576

commit v4 on v3

--- a/solution.py
+++ b/solution.py
@@ -10,6 +10,7 @@
 SWEEPS = 4
 PARTS = 4
 LATE = 4
+PLACED = 16
 LANES = 128
 HALO = 2 * SWEEPS
 MARGIN = 8
@@ -77,8 +78,7 @@
 
     lax.fori_loop(1, tiles, greet, 0)
 
-    for load in loads:
-        load.wait()
+    loads[0].wait()
     destination = dest[...]
     lane_a = lax.broadcasted_iota(jnp.int32, (LANES, 2 * LANES), 0)
     lane_b = lax.broadcasted_iota(jnp.int32, (LANES, 2 * LANES), 1)
@@ -104,6 +104,8 @@
     rank = rank.astype(jnp.int32)
     slots[0] = (destination >> 1) * blocks + (rank >> 7)
     slots[1] = (destination & 1) * LANES + (rank & (LANES - 1))
+    for load in loads[1:]:
+        load.wait()
     kind = source[...]
     factor = jnp.where(kind == 0, gain[0], jnp.where(kind == 1, gain[1], gain[2]))
     scaled = weight[...] * factor
@@ -120,8 +122,8 @@
     routed[...] = jnp.zeros(routed.shape, f32)
 
     def place(step, carry):
-        for r in range(8):
-            here = pl.ds(step * 8 + r, 1)
+        for r in range(PLACED):
+            here = pl.ds(step * PLACED + r, 1)
             lanes = slice(r * LANES, (r + 1) * LANES)
             chosen = slot_ids == slots[0, here, :]
             left_route[:, lanes] = jnp.concatenate(
@@ -135,7 +137,7 @@
         )
         return carry
 
-    lax.fori_loop(0, sounding_rows // 8, place, 0)
+    lax.fori_loop(0, sounding_rows // PLACED, place, 0)
 
     def piece(p):
         return routed[p * slot_rows : (p + 1) * slot_rows, :]
@@ -452,7 +454,7 @@
     assert lax.axis_size("col") == 2
     assert tile_rows == 64 and tile_cols <= 2048 and tile_cols % (PARTS * LANES) == 0
     count = dest_tile.shape[0]
-    assert count % (8 * LANES) == 0
+    assert count % (PLACED * LANES) == 0
     sounding_rows = count // LANES
     tiles = 2 * row_count
     capacity = 5 * count // (4 * tiles)
@@ -476,8 +478,8 @@
             pltpu.SemaphoreType.DMA((8,)),
             pltpu.VMEM((tiles, box_rows, LANES), f32),
             pltpu.VMEM((tiles, box_rows, LANES), f32),
-            pltpu.VMEM((6 * slot_rows, 8 * LANES), bf16),
-            pltpu.VMEM((2 * LANES, 8 * LANES), bf16),
+            pltpu.VMEM((6 * slot_rows, PLACED * LANES), bf16),
+            pltpu.VMEM((2 * LANES, PLACED * LANES), bf16),
             pltpu.VMEM((6 * slot_rows, 2 * LANES), f32),
             pltpu.VMEM((2, sounding_rows, LANES), jnp.int32),
             pltpu.VMEM((6, sounding_rows, LANES), f32),

time: 32.6 us -> 32 us (0.982)
  Pallas kernels: 30.6 us -> 29.9 us
    pallas_call x1, Pallas kernels: 30.6 us -> 29.9 us  [body(): call(start, dest_tile.reshape(shaped), cell_row.reshape(shaped), cell_col...]
where the time goes in v4:
time: 32 us; the launch traced here: 31.8 us
  Pallas kernels  29.9 us (93%)
  local copies, waits for them, and re-layouts  1.87 us (6%)
    pallas_call x1, Pallas kernels, body(): call(start, dest_tile.reshape(shaped), cell_row.reshape(shaped), cell_col...  29.9 us
    unnamed x1, local copies, waits for them, and re-layouts  1.87 us

profile of v4, /device:TPU:0, one launch (start us, length us, event | category | flops | bytes accessed | tf_op | source)
XLA Modules:
  0.0 31.8 jit_solution(16832091944905262923)
XLA Ops:
  0.0 29.9 %shard_map.82 = f32[64,2048]{1,0:T(8,128)} custom-call(f32[64,2048]{1,0:T(8,128)} %start.1, s32[64,128]{1,0:T(8,128)} %bitcast.6, s32[64,128]{1,0:T(8,128)} %bitcast.7, s32[64,128]{1,0:T(8,128)} %bitcast.8, s32[64,128]{1,0:T(8,128)} %bitcast.9, f32[64,128]{1,0:T(8,128)} %bitcast.10, f32[64,128]{1,0:T(8,128)} %bitcast.11, f32[3]{0:T(128)} %refs_6_.1), custom_call_target="tpu_custom_call" | custom-call | tf_op jit(solution)/shard_map/pallas_call | solution.py:509
  30.0 1.9 %copy.10 = f32[64,2048]{1,0:T(8,128)} copy(f32[64,2048]{1,0:T(8,128)} %shard_map.82) | data formatting | bytes 1048576
